TPU v7x, 128 devices: a whole 4x4x4 slice. The times are simulated.
128 devices in a mesh: row: 8 (over x_hi, z), col: 16 (over x_lo, y, core).
Axes of the slice: x: 4 (x_hi: 2, x_lo: 2; x = x_hi * 2 + x_lo), y: 4, z: 4, core: 2. Of those that a mesh axis runs over, the one named last changes fastest.
Arguments:
- pair: bfloat16 [512, 512, 128], P('row', 'col'), may hold values from -6 to 6
- cotangent: bfloat16 [512, 512, 128], P('row', 'col'), may hold values from -6 to 6
- in_gain: float32 [128], replicated, may hold values from 0.5 to 1.5
- w_in: bfloat16 [128, 640], replicated, may hold values from -0.5 to 0.5
- out_gain: float32 [128], replicated, may hold values from 0.5 to 1.5
- w_out: bfloat16 [128, 128], replicated, may hold values from -0.5 to 0.5
Outputs:
- pair_next: bfloat16 [512, 512, 128], P('row', 'col')
- pair_back: bfloat16 [512, 512, 128], P('row', 'col')
- in_gain_grad: float32 [128], replicated
- w_in_grad: float32 [128, 640], replicated
- out_gain_grad: float32 [128], replicated
- w_out_grad: float32 [128, 128], replicated
All inputs are finite; a program needn't handle non-finite values.
Results may differ from a plain program's by a relative error of at most 0.0081.
Values may be sent and summed in bfloat16 or wider, within the bound.
A program may use at most 128 MiB of HBM per device.

v0:
```python
import jax
import jax.numpy as jnp
from jax import lax
from jax.sharding import PartitionSpec as P

EPSILON = 1e-05


def layer_norm(values, scales):
    center = values - jnp.mean(values, axis=-1, keepdims=True)
    spread = jnp.mean(center * center, axis=-1, keepdims=True)
    return center * lax.rsqrt(spread + EPSILON) * scales


def project_in(pair, in_gain, w_in, hidden):
    normed = layer_norm(pair.astype(jnp.float32), in_gain).astype(jnp.bfloat16)
    project = jnp.dot(normed, w_in, preferred_element_type=jnp.float32)
    left_full = jax.nn.sigmoid(project[..., :hidden]) * project[..., hidden : 2 * hidden]
    right_full = (
        jax.nn.sigmoid(project[..., 2 * hidden : 3 * hidden])
        * project[..., 3 * hidden : 4 * hidden]
    )
    out_gate = jax.nn.sigmoid(project[..., 4 * hidden :])
    return (normed, project, left_full, right_full, out_gate)


def project_in_grad(pair, in_gain, w_in, normed, project, left_cot, right_cot, gate_cot, hidden):
    sig_left = jax.nn.sigmoid(project[..., :hidden])
    sig_right = jax.nn.sigmoid(project[..., 2 * hidden : 3 * hidden])
    sig_gate = jax.nn.sigmoid(project[..., 4 * hidden :])
    pieces = [
        left_cot * project[..., hidden : 2 * hidden] * sig_left * (1.0 - sig_left),
        left_cot * sig_left,
        right_cot * project[..., 3 * hidden : 4 * hidden] * sig_right * (1.0 - sig_right),
        right_cot * sig_right,
        gate_cot * sig_gate * (1.0 - sig_gate),
    ]
    project_cot = jnp.concatenate(pieces, axis=-1).astype(jnp.bfloat16)
    width = normed.shape[-1]
    weight_sum = jnp.dot(
        normed.reshape(-1, width).T,
        project_cot.reshape(-1, project_cot.shape[-1]),
        preferred_element_type=jnp.float32,
    )
    normed_cot = jnp.dot(project_cot, w_in.T, preferred_element_type=jnp.float32)
    unused, pullback = jax.vjp(layer_norm, pair.astype(jnp.float32), in_gain)
    pair_grad, gain_sum = pullback(normed_cot)
    return (pair_grad, gain_sum, weight_sum)


def project_out(triangle, out_gain, w_out, out_gate):
    tri_normed = layer_norm(triangle, out_gain).astype(jnp.bfloat16)
    projected = jnp.dot(tri_normed, w_out, preferred_element_type=jnp.float32)
    return (tri_normed, projected, out_gate * projected)


def project_out_grad(triangle, out_gain, w_out, out_gate, tri_normed, projected, upstream):
    gate_cot = upstream * projected
    proj_cot = (upstream * out_gate).astype(jnp.bfloat16)
    width = tri_normed.shape[-1]
    weight_sum = jnp.dot(
        tri_normed.reshape(-1, width).T,
        proj_cot.reshape(-1, proj_cot.shape[-1]),
        preferred_element_type=jnp.float32,
    )
    normed_cot = jnp.dot(proj_cot, w_out.T, preferred_element_type=jnp.float32)
    unused, pullback = jax.vjp(layer_norm, triangle, out_gain)
    tri_grad, gain_sum = pullback(normed_cot)
    return (tri_grad, gain_sum, weight_sum, gate_cot)


def on_device(pair, cotangent, in_gain, w_in, out_gain, w_out):
    hidden = out_gain.shape[0]
    row_count = pair.shape[0]
    normed, project, left_full, right_full, out_gate = project_in(pair, in_gain, w_in, hidden)
    left_act = left_full.astype(jnp.bfloat16)
    right_act = right_full.astype(jnp.bfloat16)
    right_cols = lax.all_gather(right_act, "row", axis=0, tiled=True)
    right_rows = lax.all_to_all(right_cols, "col", split_axis=0, concat_axis=1, tiled=True)
    triangle = jnp.einsum(
        "ikc,jkc->ijc",
        lax.all_gather(left_act, "col", axis=1, tiled=True),
        right_rows,
        preferred_element_type=jnp.float32,
    )
    tri_normed, projected, update = project_out(triangle, out_gain, w_out, out_gate)
    pair_next = (pair.astype(jnp.float32) + update).astype(jnp.bfloat16)
    upstream = cotangent.astype(jnp.float32)
    tri_grad, out_gain_sum, w_out_sum, gate_cot = project_out_grad(
        triangle, out_gain, w_out, out_gate, tri_normed, projected, upstream
    )
    tri_cot = tri_grad.astype(jnp.bfloat16)
    tri_wide = lax.all_gather(tri_cot, "col", axis=1, tiled=True)
    left_cot = jnp.einsum("ijc,jkc->ikc", tri_wide, right_cols, preferred_element_type=jnp.float32)
    right_cot = lax.psum_scatter(
        jnp.einsum("ijc,ikc->jkc", tri_wide, left_act, preferred_element_type=jnp.float32),
        "row",
        scatter_dimension=0,
        tiled=True,
    )
    pair_grad, in_gain_sum, w_in_sum = project_in_grad(
        pair, in_gain, w_in, normed, project, left_cot, right_cot, gate_cot, hidden
    )
    pair_back = (upstream + pair_grad).astype(jnp.bfloat16)
    totals = lax.psum((in_gain_sum, w_in_sum, out_gain_sum, w_out_sum), ("row", "col"))
    factor = 1.0 / (row_count * lax.axis_size("row"))
    return (
        pair_next,
        pair_back,
        totals[0] * factor,
        totals[1] * factor,
        totals[2] * factor,
        totals[3] * factor,
    )


def solution(mesh):
    in_specs = (P("row", "col", None), P("row", "col", None), P(), P(), P(), P())
    out_specs = (P("row", "col", None), P("row", "col", None), P(), P(), P(), P())
    return jax.shard_map(
        on_device, mesh=mesh, in_specs=in_specs, out_specs=out_specs, check_vma=False
    )
```

profile of v0, /device:TPU:1, one launch (start us, length us, event | category | flops | bytes accessed | tf_op | source)
XLA Modules:
  0.0 693.2 jit_solution(17597116386569864929)
XLA Ops:
  10.7 2.2 fusion.36
  16.4 73.7 %all-gather.4.cloned.1.call-done = bf16[512,32,128]{2,1,0:T(8,128)(2,1)} async-done(((bf16[64,32,128]{2,1,0:T(8,128)(2,1)}), bf16[512,32,128]{2,1,0:T(8,128)(2,1)}) %all-gather.4.cloned.1.call-update) | async-done | bytes 4194320 | tf_op jit(solution)/shard_map/all_gather | solution.py:78
  90.2 5.4 all-to-all-start
  99.3 74.3 %all-to-all-done = bf16[512,32,128]{2,1,0:T(8,128)(2,1)} async-done(((bf16[512,32,128]{2,1,0:T(8,128)(2,1)}), bf16[512,32,128]{2,1,0:T(8,128)(2,1)}, u32[]{:S(2)}, u32[]{:S(2)}) %all-to-all-start) | async-done | bytes 4194336 | tf_op jit(solution)/shard_map/all_to_all | solution.py:79
  173.6 5.4 copy.99
  179.0 8.0 %copy.100 = bf16[32,512,128]{1,0,2:T(8,128)(2,1)} copy(bf16[32,512,128]{2,1,0:T(8,128)(2,1)} %bitcast.66) | data formatting | bytes 8388608 | tf_op jit(solution)/shard_map/all_to_all | solution.py:79
  187.0 29.2 %copy.101 = bf16[64,512,128]{0,1,2:T(8,128)(2,1)} copy(bf16[64,512,128]{2,1,0:T(8,128)(2,1)} %all-gather.6.cloned.1.call-done) | data formatting | bytes 16777216 | tf_op jit(solution)/shard_map/all_gather | solution.py:82
  216.2 9.7 %bitcast_reduce_fusion = (f32[64,32]{0,1:T(8,128)S(1)}, f32[128,32,64]{2,1,0:T(8,128)S(1)}) fusion(bf16[32,512,128]{1,0,2:T(8,128)(2,1)} %copy.100, bf16[64,512,128]{0,1,2:T(8,128)(2,1)} %copy.101), kind=kOutput, calls=%fused_computation.2 | convolution fusion | flops 268695552 | bytes 13639680 | tf_op jit(solution)/shard_map/ikc,jkc->ijc/dot_general | solution.py:80
  227.9 2.1 add_convert_fusion
  232.1 88.2 %all-gather.8.cloned.1.call-done = bf16[64,512,128]{0,1,2:T(8,128)(2,1)} async-done(((bf16[64,32,128]{0,1,2:T(8,128)(2,1)}), bf16[64,512,128]{0,1,2:T(8,128)(2,1)}) %all-gather.8.cloned.1.call-update) | async-done | bytes 8388624 | tf_op jit(solution)/shard_map/all_gather | solution.py:93
  320.3 14.6 %fusion.53 = f32[128,32,512]{2,1,0:T(8,128)} fusion(bf16[64,32,128]{0,1,2:T(8,128)(2,1)S(1)} %copy.106, bf16[64,512,128]{0,1,2:T(8,128)(2,1)} %all-gather.8.cloned.1.call-done), kind=kOutput, calls=%fused_computation.85 | convolution fusion | flops 268435456 | bytes 17301504 | tf_op jit(solution)/shard_map/ijc,ikc->jkc/dot_general | solution.py:96
  334.9 11.0 %copy.107 = f32[128,32,512]{0,1,2:T(8,128)} copy(f32[128,32,512]{2,1,0:T(8,128)} %fusion.53) | data formatting | bytes 16777216 | tf_op jit(solution)/shard_map/ijc,ikc->jkc/dot_general | solution.py:96
  346.0 8.7 %copy.104 = bf16[512,32,128]{0,1,2:T(8,128)(2,1)} copy(bf16[512,32,128]{2,1,0:T(8,128)(2,1)} %all-gather.4.cloned.1.call-done) | data formatting | bytes 8388608 | tf_op jit(solution)/shard_map/all_gather | solution.py:78
  357.0 2.5 convolution_bitcast_fusion.1
  359.5 7.2 %fusion.52 = f32[128,32,64]{2,1,0:T(8,128)S(1)} fusion(bf16[512,32,128]{0,1,2:T(8,128)(2,1)S(1)} %copy-done.2, bf16[64,512,128]{0,1,2:T(8,128)(2,1)} %all-gather.8.cloned.1.call-done), kind=kOutput, calls=%fused_computation.84 | convolution fusion | flops 268435456 | bytes 13631488 | tf_op jit(solution)/shard_map/ijc,jkc->ikc/dot_general | solution.py:94
  366.8 2.5 copy.105
  369.3 2.4 fusion.32
  373.3 87.1 %reduce-scatter.2.cloned.1.call-done = f32[64,32,128]{2,1,0:T(8,128)} async-done(((f32[512,32,128]{2,1,0:T(8,128)}), f32[64,32,128]{2,1,0:T(8,128)}) %reduce-scatter.2.cloned.1.call-update) | async-done | bytes 1048592 | tf_op jit(solution)/shard_map/reduce_scatter | solution.py:95
  460.4 2.5 fusion.29
  464.5 2.8 fusion.33
  471.3 2.4 fusion.7
  473.9 4.3 fusion.15
  478.1 64.5 %all-reduce = (f32[128]{0:T(128)S(1)}, f32[128]{0:T(128)S(1)}) all-reduce(f32[128]{0:T(128)S(1)} %get-tuple-element.10, f32[128]{0:T(128)S(1)} %get-tuple-element.6), channel_id=1, replica_groups=mesh['row'=8,'col'=16] {'row','col'}, use_global_device_ids=true, to_apply=%region_10.0 | all-reduce | flops 256 | bytes 2048 | tf_op jit(solution)/shard_map/psum | solution.py:105
  543.2 140.4 %all-reduce.4.cloned.1.call-done = (f32[128,640]{1,0:T(8,128)}, f32[128,128]{1,0:T(8,128)}) async-done(((f32[128,640]{1,0:T(8,128)}, f32[128,128]{1,0:T(8,128)}), (f32[128,640]{1,0:T(8,128)}, f32[128,128]{1,0:T(8,128)})) %all-reduce.4.cloned.1.call-update) | async-done | bytes 393232 | tf_op jit(solution)/shard_map/psum | solution.py:105
  (76 shorter events, 28.2 us)
Async XLA Ops:
  7.2 3.5 copy-start
  7.2 83.0 %all-gather.4.cloned.1.call-start = ((), (), s32[]{:S(2)}) async-start(), calls=%async_computation.2 | async-start | bytes 4718592 | tf_op jit(solution)/shard_map/all_gather | solution.py:78
  12.9 2.7 copy-start.1
  15.6 171.3 %all-gather.6.cloned.1.call-start = ((), (), s32[]{:S(2)}) async-start(), calls=%async_computation.3 | async-start | bytes 8912896 | tf_op jit(solution)/shard_map/all_gather | solution.py:82
  16.4 79.4 %copy-start.11 = (bf16[64,32,128]{2,1,0:T(8,128)(2,1)S(1)}, bf16[64,32,128]{2,1,0:T(8,128)(2,1)}, u32[]{:S(2)}) copy-start(bf16[64,32,128]{2,1,0:T(8,128)(2,1)} %param.7) | copy-start | bytes 1572868
  16.4 79.4 %copy-start.16 = (bf16[128,128]{1,0:T(8,128)(2,1)S(1)}, bf16[128,128]{1,0:T(8,128)(2,1)}, u32[]{:S(2)}) copy-start(bf16[128,128]{1,0:T(8,128)(2,1)} %param.11) | copy-start | bytes 98308
  90.2 83.4 %all-to-all-start = ((bf16[512,32,128]{2,1,0:T(8,128)(2,1)}), bf16[512,32,128]{2,1,0:T(8,128)(2,1)}, u32[]{:S(2)}, u32[]{:S(2)}) async-start(bf16[512,32,128]{2,1,0:T(8,128)(2,1)} %all-gather.4.cloned.1.call-done), calls=%async_computation | async-start | bytes 8388608 | tf_op jit(solution)/shard_map/all_to_all | solution.py:79
  95.5 224.7 %all-gather.8.cloned.1.call-start = ((), (), s32[]{:S(2)}) async-start(), calls=%async_computation.4 | async-start | bytes 17825792 | tf_op jit(solution)/shard_map/all_gather | solution.py:93
  216.2 9.7 %copy-start.15 = (f32[128]{0:T(128)S(1)}, f32[128]{0:T(128)}, u32[]{:S(2)}) copy-start(f32[128]{0:T(128)} %param.10) | copy-start | bytes 1540
  227.9 2.4 copy-start.6
  230.1 230.3 %reduce-scatter.2.cloned.1.call-start = ((), (), s32[]{:S(2)}) async-start(), calls=%async_computation.5 | async-start | bytes 9437184 | tf_op jit(solution)/shard_map/reduce_scatter | solution.py:95
  345.9 8.8 %copy-start.7 = (bf16[64,32,128]{0,1,2:T(8,128)(2,1)S(1)}, bf16[64,32,128]{0,1,2:T(8,128)(2,1)}, u32[]{:S(2)}) copy-start(bf16[64,32,128]{0,1,2:T(8,128)(2,1)} %get-tuple-element.19) | copy-start | bytes 1572868
  345.9 11.1 %copy-start.12 = (bf16[64,32,128]{2,1,0:T(8,128)(2,1)S(1)}, bf16[64,32,128]{2,1,0:T(8,128)(2,1)}, u32[]{:S(2)}) copy-start(bf16[64,32,128]{2,1,0:T(8,128)(2,1)} %param.7) | copy-start | bytes 1572868
  345.9 337.6 %all-reduce.4.cloned.1.call-start = ((), (), s32[]{:S(2)}) async-start(), calls=%async_computation.6 | async-start | bytes 786432 | tf_op jit(solution)/shard_map/psum | solution.py:105
  356.2 0.8 copy-start.9
  357.0 2.5 copy-start.2
  369.3 2.4 copy-start.4
  460.4 2.5 copy-start.8
  460.4 4.1 copy-start.10
  460.4 4.1 copy-start.13
  464.5 2.8 copy-start.3
  464.5 2.8 copy-start.14
  471.1 2.8 copy-start.5
Sparse Core Ops, SparseCore 0:
  15.8 74.3 all-gather.3
  92.4 92.0 all-gather.5
  230.2 90.0 all-gather.7
  346.0 114.3 reduce-scatter.1
  542.8 140.7 all-reduce.3
where the time goes:
time: 694 us; the launch traced here: 693 us
  waiting for transfers between devices  464 us (67%)
  local copies, waits for them, and re-layouts  72.2 us (10%)
  blocking collectives  64.5 us (9%)
  matrix products  44.4 us (6%)
  other arithmetic  27.7 us (4%)
  between operations  14.1 us (2%)
    psum x1, waiting for transfers between devices, on_device(): lax.psum((in_gain_sum, w_in_sum, out_gain_sum, w_out_sum), ('row', 'col'))  140 us
    all_gather x1, waiting for transfers between devices, on_device(): tri_wide = lax.all_gather(tri_cot, 'col', axis=1, tiled=True)  88.2 us
    reduce_scatter x1, waiting for transfers between devices, on_device(): lax.psum_scatter(jnp.einsum('ijc,ikc->jkc', tri_wide, left_act, preferred...  87.1 us
    all_to_all x1, waiting for transfers between devices, on_device(): lax.all_to_all(right_cols, 'col', split_axis=0, concat_axis=1, tiled=True)  74.3 us
    all_gather x1, waiting for transfers between devices, on_device(): right_cols = lax.all_gather(right_act, 'row', axis=0, tiled=True)  73.7 us
    psum x1, blocking collectives, on_device(): lax.psum((in_gain_sum, w_in_sum, out_gain_sum, w_out_sum), ('row', 'col'))  64.5 us
    all_gather x1, local copies, waits for them, and re-layouts, on_device(): lax.all_gather(left_act, 'col', axis=1, tiled=True)  29.2 us
    dot_general x1, matrix products, on_device(): jnp.einsum('ijc,ikc->jkc', tri_wide, left_act, preferred_element_type=jnp...  14.6 us
  transfers between devices with their start and end apart: 6, of which 5 were waited for; matrix products, arithmetic and copies ran while one was open for 7% of the time, Pallas kernels for 0%

commit v1 on v0

v1 whole, which is shorter than its diff:
```python
import itertools

import jax
import jax.numpy as jnp
from jax import lax
from jax.experimental import pallas as pl
from jax.experimental.pallas import tpu as pltpu
from jax.sharding import PartitionSpec as P

EPSILON = 1e-05
LOGICAL = pl.DeviceIdType.LOGICAL
DEVICES = 128
CHIPS = 64
CH = 128
CELLS = 2048
CHUNK = 256
TILES = CHUNK // 128
STEPS = CELLS // CHUNK
VMEM_BYTES = 63 * 2**20
F32 = jnp.float32
BF16 = jnp.bfloat16
HOPS = sorted(itertools.product((0, 1, 2), repeat=3), key=lambda hops: (-sum(hops), hops))[:-1]


def matmul(a, b):
    return jnp.dot(a, b, preferred_element_type=F32)


def matmul_nt(a, b):
    return lax.dot_general(a, b, (((1,), (1,)), ((), ())), preferred_element_type=F32)


def parts():
    row, col = lax.axis_index("row"), lax.axis_index("col")
    x, y, z, core = (row // 4) * 2 + col // 8, (col // 2) % 4, row % 4, col % 2
    xs = [((x + d) % 4 // 2) * 64 + ((x + d) % 4 % 2) * 8 for d in range(4)]
    ys = [((y + d) % 4) * 2 for d in range(4)]
    zs = [((z + d) % 4) * 16 for d in range(4)]
    return xs, ys, zs, core


def for_chips(place, act):
    for hops in HOPS:
        ways = [(1, 3) if h == 1 else (h,) for h in hops]
        for dx, dy, dz in itertools.product(*ways):
            act(place[0][dx] + place[1][dy] + place[2][dz])


def greet(place, sibling):
    barrier = pltpu.get_barrier_semaphore()

    def signal(device):
        pl.semaphore_signal(barrier, inc=1, device_id=device, device_id_type=LOGICAL)

    def act(device):
        signal(device)
        signal(device + 1)

    for_chips(place, act)
    signal(sibling)


def remote(src, dst, send, recv, device):
    return pltpu.make_async_remote_copy(
        src_ref=src, dst_ref=dst, send_sem=send, recv_sem=recv, device_id=device, device_id_type=LOGICAL
    )


def send_to(core, place, src, dst, send, recv, me):
    def act(device):
        remote(src.at[device + core], dst.at[me], send, recv, device + core).start()

    for_chips(place, act)


def send_near(sibling, src, dst, send, recv, me):
    remote(src.at[sibling], dst.at[me], send, recv, sibling).start()
    pltpu.make_async_copy(src.at[me], dst.at[me], recv).start()


def wait_all(ref, sem):
    pltpu.make_async_copy(ref, ref, sem).wait()


def wait_sent(ref, sem):
    part = ref.at[pl.ds(0, ref.shape[0] - 1)]
    pltpu.make_async_copy(part, part, sem).wait()


def block(index):
    return pl.ds(index * 128, 128)


def cells_of(chunk):
    return pl.ds(pl.multiple_of(chunk * CHUNK, CHUNK), CHUNK)


def gather_matrix(received, perm, whole):
    rows = [
        jnp.concatenate([received[:, q_hi * 4 + q_lo].reshape(128, 128) for q_lo in range(4)], axis=1)
        for q_hi in range(4)
    ]
    moved = matmul(jnp.concatenate(rows, axis=0), perm[...]).astype(BF16)
    for q_hi in range(4):
        for i_lo in range(4):
            whole[block(i_lo), block(q_hi)] = tile(moved, q_hi, i_lo)


def scatter_matrix(whole, perm, outgoing):
    whole = whole.astype(BF16)
    rows = [
        jnp.concatenate([tile(whole, i_lo, q_hi) for i_lo in range(4)], axis=1) for q_hi in range(4)
    ]
    moved = matmul(jnp.concatenate(rows, axis=0), perm[...]).astype(BF16)
    for q_hi in range(4):
        for q_lo in range(4):
            outgoing[:, q_hi * 4 + q_lo] = tile(moved, q_hi, q_lo).reshape(8, 16, 128)


def tile(value, i, j):
    return value[i * 128 : (i + 1) * 128, j * 128 : (j + 1) * 128]


def put_tiles(spread, base, chunk, value):
    for t in range(TILES):
        spread[pl.ds(base + chunk * TILES + t, 128, stride=16), :] = value[:, t * 128 : (t + 1) * 128]


def get_tiles(spread, base, chunk):
    tiles = [spread[pl.ds(base + chunk * TILES + t, 128, stride=16), :] for t in range(TILES)]
    return jnp.concatenate(tiles, axis=1)


def put_row(rows, index, value):
    rows[pl.ds(index, 128, stride=4), :] = value


def get_row(rows, index):
    return rows[pl.ds(index, 128, stride=4), :]


def sums_scatter(place, send, recv, sums, received, total, totals, first, chip, core):
    tiles = sums.reshape(CHIPS, 8, 128)

    def act(device):
        remote(
            tiles.at[device // 2], received.at[chip], send.at[first], recv.at[first], device + core
        ).start()

    for_chips(place, act)
    pltpu.make_async_copy(tiles.at[chip], received.at[chip], recv.at[first]).start()


def sums_add(sibling, send, recv, sums, received, total, totals, first, chip, core):
    wait_all(received, recv.at[first])
    total[0] = jnp.sum(received[...], axis=0) * (1.0 / 512.0)
    swap = remote(total.at[0], total.at[1], send.at[first + 1], recv.at[first + 1], sibling)
    swap.start()
    swap.wait()
    total[2] = total[0] + total[1]


def sums_gather(place, send, recv, sums, received, total, totals, first, chip, core):
    whole = totals.reshape(CHIPS, 8, 128)

    def act(device):
        remote(total.at[2], whole.at[chip], send.at[first + 2], recv.at[first + 2], device + core).start()

    for_chips(place, act)
    pltpu.make_async_copy(total.at[2], whole.at[chip], recv.at[first + 2]).start()


def kernel(
    pair_hbm,
    cot_hbm,
    in_gain_hbm,
    w_in_hbm,
    out_gain_hbm,
    w_out_hbm,
    next_hbm,
    back_hbm,
    in_gain_hbm_out,
    w_in_hbm_out,
    out_gain_hbm_out,
    w_out_hbm_out,
    next_ref,
    back_ref,
    in_gain_out,
    w_in_out,
    out_gain_out,
    w_out_out,
    pair_ref,
    cot_ref,
    in_gain_ref,
    w_in_ref,
    out_gain_ref,
    w_out_ref,
    w_in_t,
    w_out_t,
    in_gain_t,
    out_gain_t,
    perm,
    rows_perm,
    rows_perm_t,
    pair_t,
    cot_t,
    hat,
    rstd,
    normed,
    left_a,
    left_b,
    right_a,
    right_b,
    gate,
    proj_cot,
    scaled,
    tri_hat,
    tri_normed,
    spread,
    l_out,
    l_in,
    r_out,
    r_in,
    left,
    right_raw,
    right,
    tri_out,
    tri_in,
    tc_out,
    tc_in,
    tc,
    tc_t,
    lc_out,
    lc_in,
    rc_out,
    rc_in,
    project_cot,
    early_sums,
    early_in,
    early_total,
    early_totals,
    late_sums,
    late_in,
    late_total,
    late_totals,
    load,
    store,
    send,
    recv,
):
    *place, core = parts()
    me = lax.axis_index("row") * 16 + lax.axis_index("col")
    chip = me // 2
    sibling = me + 1 - 2 * core
    loads = [
        pltpu.make_async_copy(src, dst, load.at[n])
        for n, (src, dst) in enumerate(
            (
                (pair_hbm, pair_ref),
                (w_in_hbm, w_in_ref),
                (in_gain_hbm, in_gain_ref),
                (cot_hbm, cot_ref),
                (w_out_hbm, w_out_ref),
                (out_gain_hbm, out_gain_ref),
            )
        )
    ]
    for copy in loads:
        copy.start()
    greet(place, sibling)

    a = lax.broadcasted_iota(jnp.int32, (512, 512), 0)
    b = lax.broadcasted_iota(jnp.int32, (512, 512), 1)
    swapped = ((a // 32) % 4) * 128 + (a // 128) * 32 + a % 32
    perm[...] = jnp.where(swapped == b, 1.0, 0.0).astype(BF16)
    rows_perm[...] = jnp.where((a % 4) * 128 + a // 4 == b, 1.0, 0.0).astype(BF16)
    rows_perm_t[...] = jnp.where((b % 4) * 128 + b // 4 == a, 1.0, 0.0).astype(BF16)
    for copy in loads:
        copy.wait()
    for n in range(5):
        w_in_t[block(n), :] = w_in_ref[:, block(n)].T
    w_out_t[...] = w_out_ref[...].T
    in_gain_t[...] = jnp.broadcast_to(in_gain_ref[...], (128, 128)).T
    out_gain_t[...] = jnp.broadcast_to(out_gain_ref[...], (128, 128)).T

    def project(chunk, carry):
        cells = cells_of(chunk)
        x = pair_ref[cells, :].astype(F32).T
        pair_t[:, cells] = x
        center = x - jnp.mean(x, axis=0, keepdims=True)
        inverse = lax.rsqrt(jnp.mean(center * center, axis=0, keepdims=True) + EPSILON)
        x_hat = center * inverse
        hat[:, cells] = x_hat
        rstd[:, cells] = inverse
        y = (x_hat * in_gain_t[:, :1]).astype(BF16)
        normed[:, cells] = y
        for side, (keep_a, keep_b) in enumerate(((left_a, left_b), (right_a, right_b))):
            both = matmul(w_in_t[pl.ds(side * 256, 256), :], y)
            sig = jax.nn.sigmoid(both[:128])
            act = sig * both[128:]
            keep_b[:, cells] = sig
            keep_a[:, cells] = act * (1.0 - sig)
            put_tiles(spread, side * 2048, chunk, act)
        return carry

    lax.fori_loop(0, STEPS, project, 0, unroll=2)
    r_out[...] = spread[pl.ds(2048, 2048), :].astype(BF16).reshape(128, 16, 128)
    pl.semaphore_wait(pltpu.get_barrier_semaphore(), DEVICES - 1)
    right_way = (r_out, r_in, send.at[0], recv.at[0], me)
    left_way = (l_out, l_in, send.at[1], recv.at[1], me)
    send_to(0, place, *right_way)
    l_out[...] = spread[pl.ds(0, 2048), :].astype(BF16).reshape(128, 16, 128)
    send_to(0, place, *left_way)
    send_to(1, place, *right_way)
    send_near(sibling, *right_way)
    send_to(1, place, *left_way)
    send_near(sibling, *left_way)

    def upstream(chunk, carry):
        cells = cells_of(chunk)
        sig = jax.nn.sigmoid(matmul(w_in_t[pl.ds(512, 128), :], normed[:, cells]))
        gate[:, cells] = sig
        up = cot_ref[cells, :].astype(F32).T
        cot_t[:, cells] = up
        back = (up * sig).astype(BF16)
        proj_cot[:, cells] = back
        scaled[:, cells] = matmul(w_out_ref[...], back) * out_gain_t[:, :1]
        return carry

    lax.fori_loop(0, STEPS, upstream, 0)

    wait_all(r_in, recv.at[0])
    gather_matrix(r_in.reshape(8, 16, 16, 128), perm, right_raw)
    right[...] = matmul(rows_perm[...], right_raw[...]).astype(BF16)
    wait_all(l_in, recv.at[1])
    gather_matrix(l_in.reshape(8, 16, 16, 128), perm, left)
    scatter_matrix(matmul_nt(left[...], right[...]), perm, tri_out.reshape(8, 16, 16, 128))
    way = (tri_out, tri_in, send.at[2], recv.at[2], me)
    send_to(0, place, *way)
    send_to(1, place, *way)
    send_near(sibling, *way)
    wait_all(tri_in, recv.at[2])

    spread[pl.ds(0, 2048), :] = tri_in[...].reshape(2048, 128).astype(F32)

    def middle(chunk, carry):
        cells = cells_of(chunk)
        x = get_tiles(spread, 0, chunk)
        center = x - jnp.mean(x, axis=0, keepdims=True)
        inverse = lax.rsqrt(jnp.mean(center * center, axis=0, keepdims=True) + EPSILON)
        x_hat = center * inverse
        tri_hat[:, cells] = x_hat
        grad = scaled[:, cells]
        mean = jnp.mean(grad, axis=0, keepdims=True)
        along = jnp.mean(grad * x_hat, axis=0, keepdims=True)
        put_tiles(spread, 2048, chunk, inverse * (grad - mean - x_hat * along))
        return carry

    lax.fori_loop(0, STEPS, middle, 0, unroll=4)
    tc_out[...] = spread[pl.ds(2048, 2048), :].astype(BF16).reshape(128, 16, 128)
    way = (tc_out, tc_in, send.at[3], recv.at[3], me)
    send_to(0, place, *way)
    send_to(1, place, *way)
    send_near(sibling, *way)

    def update(chunk, carry):
        cells = cells_of(chunk)
        y = (tri_hat[:, cells] * out_gain_t[:, :1]).astype(BF16)
        tri_normed[:, cells] = y
        projected = matmul(w_out_t[...], y)
        sig = gate[:, cells]
        next_ref[cells, :] = (pair_t[:, cells] + sig * projected).T.astype(BF16)
        project_cot[pl.ds(512, 128), cells] = (
            cot_t[:, cells] * projected * sig * (1.0 - sig)
        ).astype(BF16)
        return carry

    lax.fori_loop(0, STEPS, update, 0)

    early = (early_sums, early_in, early_total, early_totals, 6, chip, core)
    late = (late_sums, late_in, late_total, late_totals, 9, chip, core)
    w_out_sum = matmul_nt(tri_normed[...], proj_cot[...])
    put_row(early_sums, 0, matmul_nt(normed[...], project_cot[block(4), :]))
    for n in (1, 2, 3):
        put_row(early_sums, n, w_out_sum)
    sums_scatter(place, send, recv, *early)
    next_copy = pltpu.make_async_copy(next_ref, next_hbm, store.at[0])
    next_copy.start()
    wait_all(tc_in, recv.at[3])

    gather_matrix(tc_in.reshape(8, 16, 16, 128), perm, tc)
    scatter_matrix(matmul(tc[...], right[...]), perm, lc_out.reshape(8, 16, 16, 128))
    left_way = (lc_out, lc_in, send.at[4], recv.at[4], me)
    send_to(0, place, *left_way)
    tc_t[...] = matmul_nt(rows_perm_t[...], tc[...]).astype(BF16)
    scatter_matrix(matmul(tc_t[...], left[...]), perm, rc_out.reshape(8, 16, 16, 128))
    right_way = (rc_out, rc_in, send.at[5], recv.at[5], me)
    send_to(0, place, *right_way)
    send_to(1, place, *left_way)
    send_near(sibling, *left_way)
    send_to(1, place, *right_way)
    send_near(sibling, *right_way)

    sums_add(sibling, send, recv, *early)

    for side, (got, keep_a, keep_b) in enumerate(((lc_in, left_a, left_b), (rc_in, right_a, right_b))):
        wait_all(got, recv.at[4 + side])
        spread[pl.ds(side * 2048, 2048), :] = got[...].reshape(2048, 128).astype(F32)

        def products(chunk, carry):
            cells = cells_of(chunk)
            grad = get_tiles(spread, side * 2048, chunk)
            project_cot[pl.ds(side * 256, 128), cells] = (grad * keep_a[:, cells]).astype(BF16)
            project_cot[pl.ds(side * 256 + 128, 128), cells] = (grad * keep_b[:, cells]).astype(BF16)
            return carry

        lax.fori_loop(0, STEPS, products, 0, unroll=4)
        part = matmul_nt(normed[...], project_cot[pl.ds(side * 256, 256), :])
        put_row(late_sums, 2 * side, part[:, :128])
        put_row(late_sums, 2 * side + 1, part[:, 128:])

    sums_scatter(place, send, recv, *late)
    sums_gather(place, send, recv, *early)

    def finish(chunk, carry):
        cells = cells_of(chunk)
        grad = matmul(w_in_ref[...], project_cot[:, cells]) * in_gain_t[:, :1]
        x_hat = hat[:, cells]
        mean = jnp.mean(grad, axis=0, keepdims=True)
        along = jnp.mean(grad * x_hat, axis=0, keepdims=True)
        back = rstd[:, cells] * (grad - mean - x_hat * along)
        back_ref[cells, :] = (cot_t[:, cells] + back).T.astype(BF16)
        return carry

    lax.fori_loop(0, STEPS, finish, 0, unroll=2)
    back_copy = pltpu.make_async_copy(back_ref, back_hbm, store.at[1])
    back_copy.start()
    sums_add(sibling, send, recv, *late)
    sums_gather(place, send, recv, *late)
    wait_all(early_totals, recv.at[8])
    wait_all(late_totals, recv.at[11])

    along = jnp.zeros((128, 128), F32)
    for n in range(5):
        part = get_row(early_totals, 0) if n == 4 else get_row(late_totals, n)
        w_in_out[:, block(n)] = part
        along += part * w_in_ref[:, block(n)].astype(F32)
    in_gain_out[...] = jnp.sum((along / in_gain_t[...]).T, axis=0, keepdims=True)
    part = get_row(early_totals, 1)
    w_out_out[...] = part
    along = part * w_out_ref[...].astype(F32) / out_gain_t[...]
    out_gain_out[...] = jnp.sum(along.T, axis=0, keepdims=True)

    stores = [next_copy, back_copy] + [
        pltpu.make_async_copy(src, dst, store.at[2 + n])
        for n, (src, dst) in enumerate(
            (
                (in_gain_out, in_gain_hbm_out),
                (w_in_out, w_in_hbm_out),
                (out_gain_out, out_gain_hbm_out),
                (w_out_out, w_out_hbm_out),
            )
        )
    ]
    for copy in stores[2:]:
        copy.start()
    for copy in stores:
        copy.wait()
    wait_sent(r_out, send.at[0])
    wait_sent(l_out, send.at[1])
    wait_sent(tri_out, send.at[2])
    wait_sent(tc_out, send.at[3])
    wait_sent(lc_out, send.at[4])
    wait_sent(rc_out, send.at[5])
    for n in (6, 8, 9, 11):
        wait_sent(early_in, send.at[n])


def deliver(*refs):
    srcs, dsts, holds = refs[:6], refs[6:12], refs[12:18]
    load, store = refs[18:]
    loads = [pltpu.make_async_copy(src, hold, load.at[n]) for n, (src, hold) in enumerate(zip(srcs, holds))]
    stores = [pltpu.make_async_copy(hold, dst, store.at[n]) for n, (hold, dst) in enumerate(zip(holds, dsts))]
    for copy in loads:
        copy.start()
    for first, second in zip(loads, stores):
        first.wait()
        second.start()
    for copy in stores:
        copy.wait()


def on_device(pair, cotangent, in_gain, w_in, out_gain, w_out):
    hbm = pl.BlockSpec(memory_space=pltpu.HBM)

    def bf(*shape):
        return pltpu.VMEM(shape, BF16)

    def fl(*shape):
        return pltpu.VMEM(shape, F32)

    scratch = [
        bf(2048, 128),
        bf(2048, 128),
        fl(1, 128),
        fl(128, 640),
        fl(1, 128),
        fl(128, 128),
        bf(2048, 128),
        bf(2048, 128),
        fl(1, 128),
        bf(128, 640),
        fl(1, 128),
        bf(128, 128),
        bf(640, 128),
        bf(128, 128),
        fl(128, 128),
        fl(128, 128),
        bf(512, 512),
        bf(512, 512),
        bf(512, 512),
        fl(128, 2048),
        fl(128, 2048),
        fl(128, 2048),
        fl(1, 2048),
        bf(128, 2048),
        fl(128, 2048),
        fl(128, 2048),
        fl(128, 2048),
        fl(128, 2048),
        fl(128, 2048),
        bf(128, 2048),
        fl(128, 2048),
        fl(128, 2048),
        bf(128, 2048),
        fl(4096, 128),
        bf(128, 16, 128),
        bf(128, 16, 128),
        bf(128, 16, 128),
        bf(128, 16, 128),
        bf(512, 512),
        bf(512, 512),
        bf(512, 512),
        bf(128, 16, 128),
        bf(128, 16, 128),
        bf(128, 16, 128),
        bf(128, 16, 128),
        bf(512, 512),
        bf(512, 512),
        bf(128, 16, 128),
        bf(128, 16, 128),
        bf(128, 16, 128),
        bf(128, 16, 128),
        bf(640, 2048),
        fl(512, 128),
        fl(64, 8, 128),
        fl(3, 8, 128),
        fl(512, 128),
        fl(512, 128),
        fl(64, 8, 128),
        fl(3, 8, 128),
        fl(512, 128),
        pltpu.SemaphoreType.DMA((6,)),
        pltpu.SemaphoreType.DMA((6,)),
        pltpu.SemaphoreType.DMA((12,)),
        pltpu.SemaphoreType.DMA((12,)),
    ]
    shapes = [
        jax.ShapeDtypeStruct((CELLS, CH), BF16),
        jax.ShapeDtypeStruct((CELLS, CH), BF16),
        jax.ShapeDtypeStruct((1, CH), F32),
        jax.ShapeDtypeStruct((CH, 640), F32),
        jax.ShapeDtypeStruct((1, CH), F32),
        jax.ShapeDtypeStruct((CH, CH), F32),
    ]
    results = pl.pallas_call(
        kernel,
        out_shape=shapes,
        in_specs=[hbm] * 6,
        out_specs=[hbm] * 6,
        scratch_shapes=scratch,
        compiler_params=pltpu.CompilerParams(
            collective_id=0, has_side_effects=True, vmem_limit_bytes=VMEM_BYTES
        ),
        name="triangle_update",
    )(
        pair.reshape(CELLS, CH),
        cotangent.reshape(CELLS, CH),
        in_gain.reshape(1, CH),
        w_in,
        out_gain.reshape(1, CH),
        w_out,
    )
    pair_next, pair_back, in_gain_grad, w_in_grad, out_gain_grad, w_out_grad = pl.pallas_call(
        deliver,
        out_shape=shapes,
        in_specs=[hbm] * 6,
        out_specs=[hbm] * 6,
        scratch_shapes=[
            *(pltpu.VMEM(shape.shape, shape.dtype) for shape in shapes),
            pltpu.SemaphoreType.DMA((6,)),
            pltpu.SemaphoreType.DMA((6,)),
        ],
        compiler_params=pltpu.CompilerParams(vmem_limit_bytes=VMEM_BYTES),
        name="deliver",
    )(*results)
    return (
        pair_next.reshape(64, 32, CH),
        pair_back.reshape(64, 32, CH),
        in_gain_grad.reshape(CH),
        w_in_grad,
        out_gain_grad.reshape(CH),
        w_out_grad,
    )


def solution(mesh):
    in_specs = (P("row", "col", None), P("row", "col", None), P(), P(), P(), P())
    out_specs = (P("row", "col", None), P("row", "col", None), P(), P(), P(), P())
    return jax.shard_map(
        on_device, mesh=mesh, in_specs=in_specs, out_specs=out_specs, check_vma=False
    )
```

time: 694 us -> 77.4 us (0.11)
  waiting for transfers between devices: 464 us -> 0 us
  Pallas kernels: 0 us -> 76.7 us
  local copies, waits for them, and re-layouts: 72.2 us -> 0 us
  blocking collectives: 64.5 us -> 0 us
  matrix products: 44.4 us -> 0 us
  other arithmetic: 27.7 us -> 0 us
  between operations: 14.1 us -> 0.64 us
    all_gather x3 -> x0, waiting for transfers between devices: 162 us -> none  [the longest x1 88.2 us: on_device(): tri_wide = lax.all_gather(tri_cot, 'col', axis=1, tiled=True)]
    psum x1 -> x0, waiting for transfers between devices: 140 us -> none  [on_device(): lax.psum((in_gain_sum, w_in_sum, out_gain_sum, w_out_sum), ('row', 'col'))]
    reduce_scatter x1 -> x0, waiting for transfers between devices: 87.1 us -> none  [on_device(): lax.psum_scatter(jnp.einsum('ijc,ikc->jkc', tri_wide, left_act, preferred...]
    pallas_call x0 -> x2, Pallas kernels: none -> 76.7 us  [the longest x1 74.4 us: on_device(): pl.pallas_call(kernel, out_shape=shapes, in_specs=[hbm] * 6, out_specs=[h...]
    all_to_all x1 -> x0, waiting for transfers between devices: 74.3 us -> none  [on_device(): lax.all_to_all(right_cols, 'col', split_axis=0, concat_axis=1, tiled=True)]
    psum x1 -> x0, blocking collectives: 64.5 us -> none  [on_device(): lax.psum((in_gain_sum, w_in_sum, out_gain_sum, w_out_sum), ('row', 'col'))]
    dot_general x9 -> x0, matrix products: 44.4 us -> none  [the longest x1 14.6 us: on_device(): jnp.einsum('ijc,ikc->jkc', tri_wide, left_act, preferred_element_type=jnp...]
    all_gather x2 -> x0, local copies, waits for them, and re-layouts: 37.9 us -> none  [the longest x1 29.2 us: on_device(): lax.all_gather(left_act, 'col', axis=1, tiled=True)]
  transfers between devices with their start and end apart: 6 -> 0, of which waited for: 5 -> 0; matrix products, arithmetic and copies ran while one was open for 7% -> 0% of each run, Pallas kernels for 0% -> 0%
where the time goes in v1:
time: 77.4 us; the launch traced here: 77.3 us
  Pallas kernels  76.7 us (99%)
    pallas_call x1, Pallas kernels, on_device(): pl.pallas_call(kernel, out_shape=shapes, in_specs=[hbm] * 6, out_specs=[h...  74.4 us
    pallas_call x1, Pallas kernels, on_device(): pl.pallas_call(deliver, out_shape=shapes, in_specs=[hbm] * 6, out_specs=[...  2.24 us

profile of v1, /device:TPU:1, one launch (start us, length us, event | category | flops | bytes accessed | tf_op | source)
XLA Modules:
  0.0 77.3 jit_solution(13885063426656369323)
XLA Ops:
  0.6 74.4 %triangle_update.1 = (bf16[2048,128]{1,0:T(8,128)(2,1)}, bf16[2048,128]{1,0:T(8,128)(2,1)}, f32[1,128]{1,0:T(1,128)}, f32[128,640]{1,0:T(8,128)}, f32[1,128]{1,0:T(1,128)}, /*index=5*/f32[128,128]{1,0:T(8,128)}) custom-call(bf16[2048,128]{1,0:T(8,128)(2,1)} %bitcast.8, bf16[2048,128]{1,0:T(8,128)(2,1)} %bitcast.9, f32[1,128]{1,0:T(1,128)} %bitcast.10, ...), custom_call_target="tpu_custom_call" | custom-call | tf_op jit(solution)/shard_map/triangle_update/pallas_call | solution.py:576
  75.1 2.2 %deliver.1 = (bf16[2048,128]{1,0:T(8,128)(2,1)}, bf16[2048,128]{1,0:T(8,128)(2,1)}, f32[1,128]{1,0:T(1,128)}, f32[128,640]{1,0:T(8,128)}, f32[1,128]{1,0:T(1,128)}, /*index=5*/f32[128,128]{1,0:T(8,128)}) custom-call(bf16[2048,128]{1,0:T(8,128)(2,1)} %get-tuple-element.18.refs_0_, bf16[2048,128]{1,0:T(8,128)(2,1)} %get-tuple-element.19.refs_1_, ...), custom_call_target="tpu_custom_call" | custom-call | tf_op jit(solution)/shard_map/deliver/pallas_call | solution.py:594

commit v2 on v1

--- a/solution.py
+++ b/solution.py
@@ -179,16 +179,10 @@
     w_out_hbm,
     next_hbm,
     back_hbm,
-    in_gain_hbm_out,
-    w_in_hbm_out,
-    out_gain_hbm_out,
-    w_out_hbm_out,
+    early_totals,
+    late_totals,
     next_ref,
     back_ref,
-    in_gain_out,
-    w_in_out,
-    out_gain_out,
-    w_out_out,
     pair_ref,
     cot_ref,
     in_gain_ref,
@@ -238,11 +232,9 @@
     early_sums,
     early_in,
     early_total,
-    early_totals,
     late_sums,
     late_in,
     late_total,
-    late_totals,
     load,
     store,
     send,
@@ -303,7 +295,7 @@
             put_tiles(spread, side * 2048, chunk, act)
         return carry
 
-    lax.fori_loop(0, STEPS, project, 0, unroll=2)
+    lax.fori_loop(0, STEPS, project, 0, unroll=4)
     r_out[...] = spread[pl.ds(2048, 2048), :].astype(BF16).reshape(128, 16, 128)
     pl.semaphore_wait(pltpu.get_barrier_semaphore(), DEVICES - 1)
     right_way = (r_out, r_in, send.at[0], recv.at[0], me)
@@ -356,7 +348,7 @@
         put_tiles(spread, 2048, chunk, inverse * (grad - mean - x_hat * along))
         return carry
 
-    lax.fori_loop(0, STEPS, middle, 0, unroll=4)
+    lax.fori_loop(0, STEPS, middle, 0, unroll=True)
     tc_out[...] = spread[pl.ds(2048, 2048), :].astype(BF16).reshape(128, 16, 128)
     way = (tc_out, tc_in, send.at[3], recv.at[3], me)
     send_to(0, place, *way)
@@ -414,7 +406,7 @@
             project_cot[pl.ds(side * 256 + 128, 128), cells] = (grad * keep_b[:, cells]).astype(BF16)
             return carry
 
-        lax.fori_loop(0, STEPS, products, 0, unroll=4)
+        lax.fori_loop(0, STEPS, products, 0, unroll=True)
         part = matmul_nt(normed[...], project_cot[pl.ds(side * 256, 256), :])
         put_row(late_sums, 2 * side, part[:, :128])
         put_row(late_sums, 2 * side + 1, part[:, 128:])
@@ -440,32 +432,8 @@
     wait_all(early_totals, recv.at[8])
     wait_all(late_totals, recv.at[11])
 
-    along = jnp.zeros((128, 128), F32)
-    for n in range(5):
-        part = get_row(early_totals, 0) if n == 4 else get_row(late_totals, n)
-        w_in_out[:, block(n)] = part
-        along += part * w_in_ref[:, block(n)].astype(F32)
-    in_gain_out[...] = jnp.sum((along / in_gain_t[...]).T, axis=0, keepdims=True)
-    part = get_row(early_totals, 1)
-    w_out_out[...] = part
-    along = part * w_out_ref[...].astype(F32) / out_gain_t[...]
-    out_gain_out[...] = jnp.sum(along.T, axis=0, keepdims=True)
-
-    stores = [next_copy, back_copy] + [
-        pltpu.make_async_copy(src, dst, store.at[2 + n])
-        for n, (src, dst) in enumerate(
-            (
-                (in_gain_out, in_gain_hbm_out),
-                (w_in_out, w_in_hbm_out),
-                (out_gain_out, out_gain_hbm_out),
-                (w_out_out, w_out_hbm_out),
-            )
-        )
-    ]
-    for copy in stores[2:]:
-        copy.start()
-    for copy in stores:
-        copy.wait()
+    next_copy.wait()
+    back_copy.wait()
     wait_sent(r_out, send.at[0])
     wait_sent(l_out, send.at[1])
     wait_sent(tri_out, send.at[2])
@@ -476,16 +444,63 @@
         wait_sent(early_in, send.at[n])
 
 
-def deliver(*refs):
-    srcs, dsts, holds = refs[:6], refs[6:12], refs[12:18]
-    load, store = refs[18:]
-    loads = [pltpu.make_async_copy(src, hold, load.at[n]) for n, (src, hold) in enumerate(zip(srcs, holds))]
-    stores = [pltpu.make_async_copy(hold, dst, store.at[n]) for n, (hold, dst) in enumerate(zip(holds, dsts))]
+def deliver(
+    next_hbm,
+    back_hbm,
+    early_hbm,
+    late_hbm,
+    in_gain_hbm,
+    w_in_hbm,
+    out_gain_hbm,
+    w_out_hbm,
+    next_out,
+    back_out,
+    in_gain_grad_out,
+    w_in_grad_out,
+    out_gain_grad_out,
+    w_out_grad_out,
+    next_ref,
+    back_ref,
+    early,
+    late,
+    in_gain,
+    w_in,
+    out_gain,
+    w_out,
+    in_gain_grad,
+    w_in_grad,
+    out_gain_grad,
+    w_out_grad,
+    load,
+    store,
+):
+    sources = (early_hbm, late_hbm, in_gain_hbm, w_in_hbm, out_gain_hbm, w_out_hbm, next_hbm, back_hbm)
+    holds = (early, late, in_gain, w_in, out_gain, w_out, next_ref, back_ref)
+    loads = [pltpu.make_async_copy(src, dst, load.at[n]) for n, (src, dst) in enumerate(zip(sources, holds))]
+    results = (next_ref, back_ref, in_gain_grad, w_in_grad, out_gain_grad, w_out_grad)
+    places = (next_out, back_out, in_gain_grad_out, w_in_grad_out, out_gain_grad_out, w_out_grad_out)
+    stores = [pltpu.make_async_copy(src, dst, store.at[n]) for n, (src, dst) in enumerate(zip(results, places))]
     for copy in loads:
         copy.start()
-    for first, second in zip(loads, stores):
-        first.wait()
-        second.start()
+    for n in (0, 1):
+        loads[6 + n].wait()
+        stores[n].start()
+    for copy in loads[:6]:
+        copy.wait()
+    along = jnp.zeros((128, 128), F32)
+    for n in range(5):
+        part = get_row(early, 0) if n == 4 else get_row(late, n)
+        w_in_grad[:, block(n)] = part
+        along += part * w_in[:, block(n)].astype(F32)
+    stores[3].start()
+    part = get_row(early, 1)
+    w_out_grad[...] = part
+    stores[5].start()
+    in_gain_grad[...] = jnp.sum(along.T, axis=0, keepdims=True) / in_gain[...]
+    along = part * w_out[...].astype(F32)
+    out_gain_grad[...] = jnp.sum(along.T, axis=0, keepdims=True) / out_gain[...]
+    stores[2].start()
+    stores[4].start()
     for copy in stores:
         copy.wait()
 
@@ -502,10 +517,6 @@
     scratch = [
         bf(2048, 128),
         bf(2048, 128),
-        fl(1, 128),
-        fl(128, 640),
-        fl(1, 128),
-        fl(128, 128),
         bf(2048, 128),
         bf(2048, 128),
         fl(1, 128),
@@ -556,12 +567,10 @@
         fl(64, 8, 128),
         fl(3, 8, 128),
         fl(512, 128),
-        fl(512, 128),
         fl(64, 8, 128),
         fl(3, 8, 128),
-        fl(512, 128),
         pltpu.SemaphoreType.DMA((6,)),
-        pltpu.SemaphoreType.DMA((6,)),
+        pltpu.SemaphoreType.DMA((2,)),
         pltpu.SemaphoreType.DMA((12,)),
         pltpu.SemaphoreType.DMA((12,)),
     ]
@@ -573,37 +582,43 @@
         jax.ShapeDtypeStruct((1, CH), F32),
         jax.ShapeDtypeStruct((CH, CH), F32),
     ]
+    params = (in_gain.reshape(1, CH), w_in, out_gain.reshape(1, CH), w_out)
+    sums_shape = jax.ShapeDtypeStruct((512, 128), F32)
     results = pl.pallas_call(
         kernel,
-        out_shape=shapes,
+        out_shape=shapes[:2] + [sums_shape] * 2,
         in_specs=[hbm] * 6,
-        out_specs=[hbm] * 6,
+        out_specs=[hbm] * 4,
         scratch_shapes=scratch,
         compiler_params=pltpu.CompilerParams(
             collective_id=0, has_side_effects=True, vmem_limit_bytes=VMEM_BYTES
         ),
         name="triangle_update",
-    )(
-        pair.reshape(CELLS, CH),
-        cotangent.reshape(CELLS, CH),
-        in_gain.reshape(1, CH),
-        w_in,
-        out_gain.reshape(1, CH),
-        w_out,
-    )
+    )(pair.reshape(CELLS, CH), cotangent.reshape(CELLS, CH), *params)
     pair_next, pair_back, in_gain_grad, w_in_grad, out_gain_grad, w_out_grad = pl.pallas_call(
         deliver,
         out_shape=shapes,
-        in_specs=[hbm] * 6,
+        in_specs=[hbm] * 8,
         out_specs=[hbm] * 6,
         scratch_shapes=[
-            *(pltpu.VMEM(shape.shape, shape.dtype) for shape in shapes),
-            pltpu.SemaphoreType.DMA((6,)),
+            bf(CELLS, CH),
+            bf(CELLS, CH),
+            fl(512, 128),
+            fl(512, 128),
+            fl(1, CH),
+            bf(CH, 640),
+            fl(1, CH),
+            bf(CH, CH),
+            fl(1, CH),
+            fl(CH, 640),
+            fl(1, CH),
+            fl(CH, CH),
+            pltpu.SemaphoreType.DMA((8,)),
             pltpu.SemaphoreType.DMA((6,)),
         ],
         compiler_params=pltpu.CompilerParams(vmem_limit_bytes=VMEM_BYTES),
         name="deliver",
-    )(*results)
+    )(*results, *params)
     return (
         pair_next.reshape(64, 32, CH),
         pair_back.reshape(64, 32, CH),

time: 77.4 us -> 74.9 us (0.968)
  Pallas kernels: 76.7 us -> 74.1 us
    pallas_call x2, Pallas kernels: 76.7 us -> 74.1 us  [the longest x1 71.6 us: on_device(): pl.pallas_call(kernel, out_shape=shapes[:2] + [sums_shape] * 2, in_specs=...]
where the time goes in v2:
time: 74.9 us; the launch traced here: 74.7 us
  Pallas kernels  74.1 us (99%)
    pallas_call x1, Pallas kernels, on_device(): pl.pallas_call(kernel, out_shape=shapes[:2] + [sums_shape] * 2, in_specs=...  71.6 us
    pallas_call x1, Pallas kernels, on_device(): pl.pallas_call(deliver, out_shape=shapes, in_specs=[hbm] * 8, out_specs=[...  2.51 us

profile of v2, /device:TPU:1, one launch (start us, length us, event | category | flops | bytes accessed | tf_op | source)
XLA Modules:
  0.0 74.7 jit_solution(7172667706818218391)
XLA Ops:
  0.6 71.6 %triangle_update.1 = (bf16[2048,128]{1,0:T(8,128)(2,1)}, bf16[2048,128]{1,0:T(8,128)(2,1)}, f32[512,128]{1,0:T(8,128)}, f32[512,128]{1,0:T(8,128)}) custom-call(bf16[2048,128]{1,0:T(8,128)(2,1)} %bitcast.8, bf16[2048,128]{1,0:T(8,128)(2,1)} %bitcast.9, f32[1,128]{1,0:T(1,128)} %bitcast.10, bf16[128,640]{1,0:T(8,128)(2,1)} %w_in_hbm.3, f32[1,128]{1,0:T(1,128)} %bitcast.12, ...), custom_call_target="tpu_custom_call" | custom-call | tf_op jit(solution)/shard_map/triangle_update/pallas_call | solution.py:587
  72.2 2.5 %deliver.1 = (bf16[2048,128]{1,0:T(8,128)(2,1)}, bf16[2048,128]{1,0:T(8,128)(2,1)}, f32[1,128]{1,0:T(1,128)}, f32[128,640]{1,0:T(8,128)}, f32[1,128]{1,0:T(1,128)}, /*index=5*/f32[128,128]{1,0:T(8,128)}) custom-call(bf16[2048,128]{1,0:T(8,128)(2,1)} %get-tuple-element.16.next_hbm, bf16[2048,128]{1,0:T(8,128)(2,1)} %get-tuple-element.17.back_hbm, ...), custom_call_target="tpu_custom_call" | custom-call | tf_op jit(solution)/shard_map/deliver/pallas_call | solution.py:598

commit v3 on v2

--- a/solution.py
+++ b/solution.py
@@ -261,19 +261,11 @@
         copy.start()
     greet(place, sibling)
 
-    a = lax.broadcasted_iota(jnp.int32, (512, 512), 0)
-    b = lax.broadcasted_iota(jnp.int32, (512, 512), 1)
-    swapped = ((a // 32) % 4) * 128 + (a // 128) * 32 + a % 32
-    perm[...] = jnp.where(swapped == b, 1.0, 0.0).astype(BF16)
-    rows_perm[...] = jnp.where((a % 4) * 128 + a // 4 == b, 1.0, 0.0).astype(BF16)
-    rows_perm_t[...] = jnp.where((b % 4) * 128 + b // 4 == a, 1.0, 0.0).astype(BF16)
-    for copy in loads:
+    for copy in loads[:3]:
         copy.wait()
     for n in range(5):
         w_in_t[block(n), :] = w_in_ref[:, block(n)].T
-    w_out_t[...] = w_out_ref[...].T
     in_gain_t[...] = jnp.broadcast_to(in_gain_ref[...], (128, 128)).T
-    out_gain_t[...] = jnp.broadcast_to(out_gain_ref[...], (128, 128)).T
 
     def project(chunk, carry):
         cells = cells_of(chunk)
@@ -295,7 +287,7 @@
             put_tiles(spread, side * 2048, chunk, act)
         return carry
 
-    lax.fori_loop(0, STEPS, project, 0, unroll=4)
+    lax.fori_loop(0, STEPS, project, 0, unroll=True)
     r_out[...] = spread[pl.ds(2048, 2048), :].astype(BF16).reshape(128, 16, 128)
     pl.semaphore_wait(pltpu.get_barrier_semaphore(), DEVICES - 1)
     right_way = (r_out, r_in, send.at[0], recv.at[0], me)
@@ -308,6 +300,17 @@
     send_to(1, place, *left_way)
     send_near(sibling, *left_way)
 
+    a = lax.broadcasted_iota(jnp.int32, (512, 512), 0)
+    b = lax.broadcasted_iota(jnp.int32, (512, 512), 1)
+    swapped = ((a // 32) % 4) * 128 + (a // 128) * 32 + a % 32
+    perm[...] = jnp.where(swapped == b, 1.0, 0.0).astype(BF16)
+    rows_perm[...] = jnp.where((a % 4) * 128 + a // 4 == b, 1.0, 0.0).astype(BF16)
+    rows_perm_t[...] = jnp.where((b % 4) * 128 + b // 4 == a, 1.0, 0.0).astype(BF16)
+    for copy in loads[3:]:
+        copy.wait()
+    w_out_t[...] = w_out_ref[...].T
+    out_gain_t[...] = jnp.broadcast_to(out_gain_ref[...], (128, 128)).T
+
     def upstream(chunk, carry):
         cells = cells_of(chunk)
         sig = jax.nn.sigmoid(matmul(w_in_t[pl.ds(512, 128), :], normed[:, cells]))
@@ -319,7 +322,7 @@
         scaled[:, cells] = matmul(w_out_ref[...], back) * out_gain_t[:, :1]
         return carry
 
-    lax.fori_loop(0, STEPS, upstream, 0)
+    lax.fori_loop(0, STEPS, upstream, 0, unroll=True)
 
     wait_all(r_in, recv.at[0])
     gather_matrix(r_in.reshape(8, 16, 16, 128), perm, right_raw)
@@ -367,7 +370,7 @@
         ).astype(BF16)
         return carry
 
-    lax.fori_loop(0, STEPS, update, 0)
+    lax.fori_loop(0, STEPS, update, 0, unroll=True)
 
     early = (early_sums, early_in, early_total, early_totals, 6, chip, core)
     late = (late_sums, late_in, late_total, late_totals, 9, chip, core)
@@ -424,7 +427,7 @@
         back_ref[cells, :] = (cot_t[:, cells] + back).T.astype(BF16)
         return carry
 
-    lax.fori_loop(0, STEPS, finish, 0, unroll=2)
+    lax.fori_loop(0, STEPS, finish, 0, unroll=True)
     back_copy = pltpu.make_async_copy(back_ref, back_hbm, store.at[1])
     back_copy.start()
     sums_add(sibling, send, recv, *late)

time: 74.9 us -> 75.4 us (level)
  no operation moved by 1% of the time
where the time goes in v3:
time: 75.4 us; the launch traced here: 75.2 us
  Pallas kernels  74.4 us (99%)
  between operations  0.8 us (1%)
    pallas_call x1, Pallas kernels, on_device(): pl.pallas_call(kernel, out_shape=shapes[:2] + [sums_shape] * 2, in_specs=...  71.9 us
    pallas_call x1, Pallas kernels, on_device(): pl.pallas_call(deliver, out_shape=shapes, in_specs=[hbm] * 8, out_specs=[...  2.51 us

profile of v3, /device:TPU:1, one launch (start us, length us, event | category | flops | bytes accessed | tf_op | source)
XLA Modules:
  0.0 75.2 jit_solution(1929453770931260977)
XLA Ops:
  0.6 71.9 %triangle_update.1 = (bf16[2048,128]{1,0:T(8,128)(2,1)}, bf16[2048,128]{1,0:T(8,128)(2,1)}, f32[512,128]{1,0:T(8,128)}, f32[512,128]{1,0:T(8,128)}) custom-call(bf16[2048,128]{1,0:T(8,128)(2,1)} %bitcast.8, bf16[2048,128]{1,0:T(8,128)(2,1)} %bitcast.9, f32[1,128]{1,0:T(1,128)} %bitcast.10, bf16[128,640]{1,0:T(8,128)(2,1)} %w_in_hbm.3, f32[1,128]{1,0:T(1,128)} %bitcast.12, ...), custom_call_target="tpu_custom_call" | custom-call | tf_op jit(solution)/shard_map/triangle_update/pallas_call | solution.py:590
  72.5 2.5 %deliver.1 = (bf16[2048,128]{1,0:T(8,128)(2,1)}, bf16[2048,128]{1,0:T(8,128)(2,1)}, f32[1,128]{1,0:T(1,128)}, f32[128,640]{1,0:T(8,128)}, f32[1,128]{1,0:T(1,128)}, /*index=5*/f32[128,128]{1,0:T(8,128)}) custom-call(bf16[2048,128]{1,0:T(8,128)(2,1)} %get-tuple-element.16.next_hbm, bf16[2048,128]{1,0:T(8,128)(2,1)} %get-tuple-element.17.back_hbm, ...), custom_call_target="tpu_custom_call" | custom-call | tf_op jit(solution)/shard_map/deliver/pallas_call | solution.py:601

commit v4 on v3

--- a/solution.py
+++ b/solution.py
@@ -139,35 +139,60 @@
     return rows[pl.ds(index, 128, stride=4), :]
 
 
-def sums_scatter(place, send, recv, sums, received, total, totals, first, chip, core):
+def sums_scatter(place, send, recv, sums, received, total, totals, first, me):
     tiles = sums.reshape(CHIPS, 8, 128)
+    own = tiles.at[me // 2]
 
     def act(device):
+        chip = device // 2
         remote(
-            tiles.at[device // 2], received.at[chip], send.at[first], recv.at[first], device + core
+            tiles.at[chip], received.at[me], send.at[first], recv.at[first], device + chip % 2
         ).start()
 
     for_chips(place, act)
-    pltpu.make_async_copy(tiles.at[chip], received.at[chip], recv.at[first]).start()
-
-
-def sums_add(sibling, send, recv, sums, received, total, totals, first, chip, core):
-    wait_all(received, recv.at[first])
-    total[0] = jnp.sum(received[...], axis=0) * (1.0 / 512.0)
-    swap = remote(total.at[0], total.at[1], send.at[first + 1], recv.at[first + 1], sibling)
-    swap.start()
-    swap.wait()
-    total[2] = total[0] + total[1]
-
-
-def sums_gather(place, send, recv, sums, received, total, totals, first, chip, core):
+
+    @pl.when(me // 2 % 2 == me % 2)
+    def _():
+        pltpu.make_async_copy(own, received.at[me], recv.at[first]).start()
+
+    @pl.when(me // 2 % 2 != me % 2)
+    def _():
+        device = me + 1 - 2 * (me % 2)
+        remote(own, received.at[me], send.at[first + 1], recv.at[first], device).start()
+
+
+def sums_gather(place, send, recv, sums, received, total, totals, first, me):
     whole = totals.reshape(CHIPS, 8, 128)
-
-    def act(device):
-        remote(total.at[2], whole.at[chip], send.at[first + 2], recv.at[first + 2], device + core).start()
-
-    for_chips(place, act)
-    pltpu.make_async_copy(total.at[2], whole.at[chip], recv.at[first + 2]).start()
+    chip = me // 2
+
+    @pl.when(chip % 2 == me % 2)
+    def _():
+        wait_all(received, recv.at[first])
+        total[...] = jnp.sum(received[...], axis=0) * (1.0 / 512.0)
+
+        def act(device):
+            for core in range(2):
+                remote(
+                    total, whole.at[chip], send.at[first + 2], recv.at[first + 2], device + core
+                ).start()
+
+        for_chips(place, act)
+        sibling = me + 1 - 2 * (me % 2)
+        remote(total, whole.at[chip], send.at[first + 2], recv.at[first + 2], sibling).start()
+        pltpu.make_async_copy(total, whole.at[chip], recv.at[first + 2]).start()
+
+
+def sums_sent(send, sums, received, total, totals, first, me):
+    tiles = sums.reshape(CHIPS, 8, 128)
+    wait_sent(tiles, send.at[first])
+
+    @pl.when(me // 2 % 2 == me % 2)
+    def _():
+        wait_sent(received, send.at[first + 2])
+
+    @pl.when(me // 2 % 2 != me % 2)
+    def _():
+        wait_all(total, send.at[first + 1])
 
 
 def kernel(
@@ -242,7 +267,6 @@
 ):
     *place, core = parts()
     me = lax.axis_index("row") * 16 + lax.axis_index("col")
-    chip = me // 2
     sibling = me + 1 - 2 * core
     loads = [
         pltpu.make_async_copy(src, dst, load.at[n])
@@ -287,7 +311,7 @@
             put_tiles(spread, side * 2048, chunk, act)
         return carry
 
-    lax.fori_loop(0, STEPS, project, 0, unroll=True)
+    lax.fori_loop(0, STEPS, project, 0, unroll=4)
     r_out[...] = spread[pl.ds(2048, 2048), :].astype(BF16).reshape(128, 16, 128)
     pl.semaphore_wait(pltpu.get_barrier_semaphore(), DEVICES - 1)
     right_way = (r_out, r_in, send.at[0], recv.at[0], me)
@@ -322,7 +346,7 @@
         scaled[:, cells] = matmul(w_out_ref[...], back) * out_gain_t[:, :1]
         return carry
 
-    lax.fori_loop(0, STEPS, upstream, 0, unroll=True)
+    lax.fori_loop(0, STEPS, upstream, 0)
 
     wait_all(r_in, recv.at[0])
     gather_matrix(r_in.reshape(8, 16, 16, 128), perm, right_raw)
@@ -370,10 +394,10 @@
         ).astype(BF16)
         return carry
 
-    lax.fori_loop(0, STEPS, update, 0, unroll=True)
-
-    early = (early_sums, early_in, early_total, early_totals, 6, chip, core)
-    late = (late_sums, late_in, late_total, late_totals, 9, chip, core)
+    lax.fori_loop(0, STEPS, update, 0)
+
+    early = (early_sums, early_in, early_total, early_totals, 6, me)
+    late = (late_sums, late_in, late_total, late_totals, 9, me)
     w_out_sum = matmul_nt(tri_normed[...], proj_cot[...])
     put_row(early_sums, 0, matmul_nt(normed[...], project_cot[block(4), :]))
     for n in (1, 2, 3):
@@ -396,8 +420,6 @@
     send_to(1, place, *right_way)
     send_near(sibling, *right_way)
 
-    sums_add(sibling, send, recv, *early)
-
     for side, (got, keep_a, keep_b) in enumerate(((lc_in, left_a, left_b), (rc_in, right_a, right_b))):
         wait_all(got, recv.at[4 + side])
         spread[pl.ds(side * 2048, 2048), :] = got[...].reshape(2048, 128).astype(F32)
@@ -427,10 +449,9 @@
         back_ref[cells, :] = (cot_t[:, cells] + back).T.astype(BF16)
         return carry
 
-    lax.fori_loop(0, STEPS, finish, 0, unroll=True)
+    lax.fori_loop(0, STEPS, finish, 0, unroll=2)
     back_copy = pltpu.make_async_copy(back_ref, back_hbm, store.at[1])
     back_copy.start()
-    sums_add(sibling, send, recv, *late)
     sums_gather(place, send, recv, *late)
     wait_all(early_totals, recv.at[8])
     wait_all(late_totals, recv.at[11])
@@ -443,8 +464,8 @@
     wait_sent(tc_out, send.at[3])
     wait_sent(lc_out, send.at[4])
     wait_sent(rc_out, send.at[5])
-    for n in (6, 8, 9, 11):
-        wait_sent(early_in, send.at[n])
+    sums_sent(send, *early)
+    sums_sent(send, *late)
 
 
 def deliver(
@@ -567,11 +588,11 @@
         bf(128, 16, 128),
         bf(640, 2048),
         fl(512, 128),
-        fl(64, 8, 128),
-        fl(3, 8, 128),
+        fl(128, 8, 128),
+        fl(8, 128),
         fl(512, 128),
-        fl(64, 8, 128),
-        fl(3, 8, 128),
+        fl(128, 8, 128),
+        fl(8, 128),
         pltpu.SemaphoreType.DMA((6,)),
         pltpu.SemaphoreType.DMA((2,)),
         pltpu.SemaphoreType.DMA((12,)),

time: 75.4 us -> 75.6 us (level)
  no operation moved by 1% of the time
where the time goes in v4:
time: 75.6 us; the launch traced here: 75.5 us
  Pallas kernels  74.7 us (99%)
  between operations  0.8 us (1%)
    pallas_call x1, Pallas kernels, on_device(): pl.pallas_call(kernel, out_shape=shapes[:2] + [sums_shape] * 2, in_specs=...  72.2 us
    pallas_call x1, Pallas kernels, on_device(): pl.pallas_call(deliver, out_shape=shapes, in_specs=[hbm] * 8, out_specs=[...  2.51 us

profile of v4, /device:TPU:1, one launch (start us, length us, event | category | flops | bytes accessed | tf_op | source)
XLA Modules:
  0.0 75.5 jit_solution(12009709106227412055)
XLA Ops:
  0.6 72.2 %triangle_update.1 = (bf16[2048,128]{1,0:T(8,128)(2,1)}, bf16[2048,128]{1,0:T(8,128)(2,1)}, f32[512,128]{1,0:T(8,128)}, f32[512,128]{1,0:T(8,128)}) custom-call(bf16[2048,128]{1,0:T(8,128)(2,1)} %bitcast.8, bf16[2048,128]{1,0:T(8,128)(2,1)} %bitcast.9, f32[1,128]{1,0:T(1,128)} %bitcast.10, bf16[128,640]{1,0:T(8,128)(2,1)} %w_in_hbm.3, f32[1,128]{1,0:T(1,128)} %bitcast.12, ...), custom_call_target="tpu_custom_call" | custom-call | tf_op jit(solution)/shard_map/triangle_update/pallas_call | solution.py:611
  72.8 2.5 %deliver.1 = (bf16[2048,128]{1,0:T(8,128)(2,1)}, bf16[2048,128]{1,0:T(8,128)(2,1)}, f32[1,128]{1,0:T(1,128)}, f32[128,640]{1,0:T(8,128)}, f32[1,128]{1,0:T(1,128)}, /*index=5*/f32[128,128]{1,0:T(8,128)}) custom-call(bf16[2048,128]{1,0:T(8,128)(2,1)} %get-tuple-element.16.next_hbm, bf16[2048,128]{1,0:T(8,128)(2,1)} %get-tuple-element.17.back_hbm, ...), custom_call_target="tpu_custom_call" | custom-call | tf_op jit(solution)/shard_map/deliver/pallas_call | solution.py:622

commit v5 on v3

--- a/solution.py
+++ b/solution.py
@@ -287,7 +287,7 @@
             put_tiles(spread, side * 2048, chunk, act)
         return carry
 
-    lax.fori_loop(0, STEPS, project, 0, unroll=True)
+    lax.fori_loop(0, STEPS, project, 0, unroll=4)
     r_out[...] = spread[pl.ds(2048, 2048), :].astype(BF16).reshape(128, 16, 128)
     pl.semaphore_wait(pltpu.get_barrier_semaphore(), DEVICES - 1)
     right_way = (r_out, r_in, send.at[0], recv.at[0], me)
@@ -322,7 +322,7 @@
         scaled[:, cells] = matmul(w_out_ref[...], back) * out_gain_t[:, :1]
         return carry
 
-    lax.fori_loop(0, STEPS, upstream, 0, unroll=True)
+    lax.fori_loop(0, STEPS, upstream, 0)
 
     wait_all(r_in, recv.at[0])
     gather_matrix(r_in.reshape(8, 16, 16, 128), perm, right_raw)
@@ -370,7 +370,7 @@
         ).astype(BF16)
         return carry
 
-    lax.fori_loop(0, STEPS, update, 0, unroll=True)
+    lax.fori_loop(0, STEPS, update, 0)
 
     early = (early_sums, early_in, early_total, early_totals, 6, chip, core)
     late = (late_sums, late_in, late_total, late_totals, 9, chip, core)
@@ -427,7 +427,7 @@
         back_ref[cells, :] = (cot_t[:, cells] + back).T.astype(BF16)
         return carry
 
-    lax.fori_loop(0, STEPS, finish, 0, unroll=True)
+    lax.fori_loop(0, STEPS, finish, 0, unroll=2)
     back_copy = pltpu.make_async_copy(back_ref, back_hbm, store.at[1])
     back_copy.start()
     sums_add(sibling, send, recv, *late)

time: 75.4 us -> 75.3 us (level)
  no operation moved by 1% of the time
where the time goes in v5:
time: 75.3 us; the launch traced here: 75.1 us
  Pallas kernels  74.3 us (99%)
  between operations  0.8 us (1%)
    pallas_call x1, Pallas kernels, on_device(): pl.pallas_call(kernel, out_shape=shapes[:2] + [sums_shape] * 2, in_specs=...  71.8 us
    pallas_call x1, Pallas kernels, on_device(): pl.pallas_call(deliver, out_shape=shapes, in_specs=[hbm] * 8, out_specs=[...  2.51 us

profile of v5, /device:TPU:1, one launch (start us, length us, event | category | flops | bytes accessed | tf_op | source)
XLA Modules:
  0.0 75.1 jit_solution(2914861856091957096)
XLA Ops:
  0.6 71.8 %triangle_update.1 = (bf16[2048,128]{1,0:T(8,128)(2,1)}, bf16[2048,128]{1,0:T(8,128)(2,1)}, f32[512,128]{1,0:T(8,128)}, f32[512,128]{1,0:T(8,128)}) custom-call(bf16[2048,128]{1,0:T(8,128)(2,1)} %bitcast.8, bf16[2048,128]{1,0:T(8,128)(2,1)} %bitcast.9, f32[1,128]{1,0:T(1,128)} %bitcast.10, bf16[128,640]{1,0:T(8,128)(2,1)} %w_in_hbm.3, f32[1,128]{1,0:T(1,128)} %bitcast.12, ...), custom_call_target="tpu_custom_call" | custom-call | tf_op jit(solution)/shard_map/triangle_update/pallas_call | solution.py:590
  72.4 2.5 %deliver.1 = (bf16[2048,128]{1,0:T(8,128)(2,1)}, bf16[2048,128]{1,0:T(8,128)(2,1)}, f32[1,128]{1,0:T(1,128)}, f32[128,640]{1,0:T(8,128)}, f32[1,128]{1,0:T(1,128)}, /*index=5*/f32[128,128]{1,0:T(8,128)}) custom-call(bf16[2048,128]{1,0:T(8,128)(2,1)} %get-tuple-element.16.next_hbm, bf16[2048,128]{1,0:T(8,128)(2,1)} %get-tuple-element.17.back_hbm, ...), custom_call_target="tpu_custom_call" | custom-call | tf_op jit(solution)/shard_map/deliver/pallas_call | solution.py:601

commit v6 on v2

--- a/solution.py
+++ b/solution.py
@@ -412,7 +412,6 @@
         put_row(late_sums, 2 * side + 1, part[:, 128:])
 
     sums_scatter(place, send, recv, *late)
-    sums_gather(place, send, recv, *early)
 
     def finish(chunk, carry):
         cells = cells_of(chunk)
@@ -427,6 +426,7 @@
     lax.fori_loop(0, STEPS, finish, 0, unroll=2)
     back_copy = pltpu.make_async_copy(back_ref, back_hbm, store.at[1])
     back_copy.start()
+    sums_gather(place, send, recv, *early)
     sums_add(sibling, send, recv, *late)
     sums_gather(place, send, recv, *late)
     wait_all(early_totals, recv.at[8])

time: 74.9 us -> 75.2 us (level)
  no operation moved by 1% of the time
where the time goes in v6:
time: 75.2 us; the launch traced here: 74.9 us
  Pallas kernels  74.3 us (99%)
    pallas_call x1, Pallas kernels, on_device(): pl.pallas_call(kernel, out_shape=shapes[:2] + [sums_shape] * 2, in_specs=...  71.8 us
    pallas_call x1, Pallas kernels, on_device(): pl.pallas_call(deliver, out_shape=shapes, in_specs=[hbm] * 8, out_specs=[...  2.51 us

profile of v6, /device:TPU:1, one launch (start us, length us, event | category | flops | bytes accessed | tf_op | source)
XLA Modules:
  0.0 74.9 jit_solution(11392507437251720178)
XLA Ops:
  0.6 71.8 %triangle_update.1 = (bf16[2048,128]{1,0:T(8,128)(2,1)}, bf16[2048,128]{1,0:T(8,128)(2,1)}, f32[512,128]{1,0:T(8,128)}, f32[512,128]{1,0:T(8,128)}) custom-call(bf16[2048,128]{1,0:T(8,128)(2,1)} %bitcast.8, bf16[2048,128]{1,0:T(8,128)(2,1)} %bitcast.9, f32[1,128]{1,0:T(1,128)} %bitcast.10, bf16[128,640]{1,0:T(8,128)(2,1)} %w_in_hbm.3, f32[1,128]{1,0:T(1,128)} %bitcast.12, ...), custom_call_target="tpu_custom_call" | custom-call | tf_op jit(solution)/shard_map/triangle_update/pallas_call | solution.py:587
  72.4 2.5 %deliver.1 = (bf16[2048,128]{1,0:T(8,128)(2,1)}, bf16[2048,128]{1,0:T(8,128)(2,1)}, f32[1,128]{1,0:T(1,128)}, f32[128,640]{1,0:T(8,128)}, f32[1,128]{1,0:T(1,128)}, /*index=5*/f32[128,128]{1,0:T(8,128)}) custom-call(bf16[2048,128]{1,0:T(8,128)(2,1)} %get-tuple-element.16.next_hbm, bf16[2048,128]{1,0:T(8,128)(2,1)} %get-tuple-element.17.back_hbm, ...), custom_call_target="tpu_custom_call" | custom-call | tf_op jit(solution)/shard_map/deliver/pallas_call | solution.py:598
